TPU v7x, 32 devices: a whole 2x2x4 slice. The times are simulated.
32 devices in a mesh: gx: 8 (over z, y), gy: 4 (over x, core).
Axes of the slice: x: 2, y: 2, z: 4, core: 2. Of those that a mesh axis runs over, the one named last changes fastest.
Arguments:
- features: float32 [8192, 1024], P(('gx', 'gy')), may hold values from -6 to 6
- labels: int32 [32], replicated, may hold values from 0 to 1, as said below
- rounds: int32 [2], replicated, may hold values from 1 to 31, as said below
Outputs:
- feature_grad: float32 [8192, 1024], P(('gx', 'gy'))
Inputs may be any that keep to these rules, and one draw needn't show every extreme that they name: Each of the two values labels some block. `rounds`: 2 different nonzero masks, one of which flips every bit of the block index.
All inputs are finite; a program needn't handle non-finite values.
Results may differ from a plain program's by a relative error of at most 0.0003.
Values sent between devices are 32-bit elements; how exact they have to be, the bound alone decides.
A program may use at most 64 MiB of HBM per device.

v0:
```python
import jax
import jax.numpy as jnp
from jax import lax
from jax.sharding import PartitionSpec as P


def pair_weight(label_own, label_other, real_rows, fake_rows, loss_scale):
    both_real = loss_scale / (real_rows * (real_rows - 1.0))
    both_fake = loss_scale / (fake_rows * (fake_rows - 1.0))
    mixed = -loss_scale / (real_rows * fake_rows)
    same = label_own == label_other
    return jnp.where(same, jnp.where(label_own == 1, both_real, both_fake), mixed)


def tile_grad(own_rows, partner, weight, skip_diag):
    row_count, feat_width = own_rows.shape
    root_width = jnp.sqrt(jnp.float32(feat_width))
    scores = jnp.dot(own_rows, partner.T, precision=lax.Precision.HIGHEST) / root_width
    coefficient = weight * (6.0 / root_width) * (scores + 1.0) ** 2
    if skip_diag:
        coefficient = jnp.where(jnp.eye(row_count, dtype=bool), jnp.float32(0.0), coefficient)
    return jnp.dot(coefficient, partner, precision=lax.Precision.HIGHEST)


def pick_pieces(spread, offset, peers):
    pieces = spread.reshape(peers, -1, spread.shape[1])
    source_order = jnp.bitwise_xor(jnp.arange(peers, dtype=jnp.int32), offset)
    return jnp.take(pieces, source_order, axis=0)


def fetch_across(block, offset):
    peers = lax.axis_size("gx")
    spread = lax.all_to_all(block, "gx", split_axis=0, concat_axis=0, tiled=True)
    chosen = pick_pieces(spread, offset, peers).reshape(block.shape)
    return lax.all_to_all(chosen, "gx", split_axis=0, concat_axis=0, tiled=True)


def fetch_down(block, offset):
    peers = lax.axis_size("gy")
    spread = lax.all_to_all(block, "gy", split_axis=0, concat_axis=0, tiled=True)
    chosen = pick_pieces(spread, offset, peers).reshape(block.shape)
    return lax.all_to_all(chosen, "gy", split_axis=0, concat_axis=0, tiled=True)


def on_device(features, labels, rounds):
    row_count = features.shape[0]
    down_size = lax.axis_size("gy")
    all_rows = row_count * lax.axis_size("gx") * down_size
    own_block = lax.axis_index("gx") * down_size + lax.axis_index("gy")
    real_rows = jnp.float32(row_count) * jnp.sum(labels).astype(jnp.float32)
    fake_rows = jnp.float32(all_rows) - real_rows
    loss_scale = float(all_rows) * float(all_rows) / 16.0
    label_own = labels[own_block]
    gradient = tile_grad(
        features,
        features,
        pair_weight(label_own, label_own, real_rows, fake_rows, loss_scale),
        True,
    )
    round_total = rounds.shape[0]
    high_parts = [rounds[index] // down_size for index in range(round_total)]
    low_parts = [rounds[index] % down_size for index in range(round_total)]
    crossed = [fetch_across(features, high_parts[index]) for index in range(round_total)]
    partners = [fetch_down(crossed[index], low_parts[index]) for index in range(round_total)]
    for round_index in range(round_total):
        partner_id = jnp.bitwise_xor(own_block, rounds[round_index])
        weight = pair_weight(label_own, labels[partner_id], real_rows, fake_rows, loss_scale)
        gradient = gradient + tile_grad(features, partners[round_index], weight, False)
    return gradient


def solution(mesh):
    in_specs = (P(("gx", "gy"), None), P(), P())
    out_specs = P(("gx", "gy"), None)
    return jax.shard_map(
        on_device, mesh=mesh, in_specs=in_specs, out_specs=out_specs, check_vma=False
    )
```

profile of v0, /device:TPU:9, one launch (start us, length us, event | category | flops | bytes accessed | tf_op | source)
XLA Modules:
  0.0 166.9 jit_solution(9367597713439488826)
XLA Ops:
  0.0 0.0 copy-start.4
  0.0 5.9 %all-to-all-start = ((f32[8,32,1024]{2,1,0:T(8,128)}), f32[8,32,1024]{2,1,0:T(8,128)S(1)}, u32[]{:S(2)}, u32[]{:S(2)}) async-start(f32[8,32,1024]{2,1,0:T(8,128)} %bitcast.22), calls=%async_computation | async-start | bytes 2097152 | tf_op jit(solution)/shard_map/all_to_all | solution.py:33
  5.9 0.0 copy-done.4
  5.9 0.7 fusion.11
  9.1 19.7 %all-to-all-done = f32[8,32,1024]{2,1,0:T(8,128)S(1)} async-done(((f32[8,32,1024]{2,1,0:T(8,128)}), f32[8,32,1024]{2,1,0:T(8,128)S(1)}, u32[]{:S(2)}, u32[]{:S(2)}) %all-to-all-start) | async-done | bytes 1048608 | tf_op jit(solution)/shard_map/all_to_all | solution.py:33
  28.8 0.6 gather_fusion
  29.4 1.2 broadcast_select_fusion.3
  30.5 6.6 %all-to-all-start.1 = ((f32[8,32,1024]{2,1,0:T(8,128)}), f32[8,32,1024]{2,1,0:T(8,128)S(1)}, u32[]{:S(2)}, u32[]{:S(2)}) async-start(f32[8,32,1024]{2,1,0:T(8,128)} %broadcast_select_fusion.3), calls=%async_computation.1 | async-start | bytes 2097152 | tf_op jit(solution)/shard_map/all_to_all | solution.py:35
  40.0 0.6 gather_fusion.2
  40.6 0.2 broadcast_select_fusion.2
  40.8 19.7 %all-to-all-done.1 = f32[8,32,1024]{2,1,0:T(8,128)S(1)} async-done(((f32[8,32,1024]{2,1,0:T(8,128)}), f32[8,32,1024]{2,1,0:T(8,128)S(1)}, u32[]{:S(2)}, u32[]{:S(2)}) %all-to-all-start.1) | async-done | bytes 1048608 | tf_op jit(solution)/shard_map/all_to_all | solution.py:35
  60.5 30.1 %all_to_all.58 = f32[8,32,1024]{2,1,0:T(8,128)} all-to-all(f32[8,32,1024]{2,1,0:T(8,128)S(1)} %broadcast_select_fusion.2), channel_id=1, replica_groups=mesh['gx'=8,'gy'=4] {'gx'}, dimensions={0} | all-to-all | bytes 2097152 | tf_op jit(solution)/shard_map/all_to_all | solution.py:35
  90.6 18.1 %all_to_all.59 = f32[4,64,1024]{2,1,0:T(8,128)S(1)} all-to-all(f32[4,64,1024]{2,1,0:T(8,128)S(1)} %bitcast.27), channel_id=1, replica_groups=mesh['gx'=8,'gy'=4] {'gy'}, dimensions={0} | all-to-all | bytes 2097152 | tf_op jit(solution)/shard_map/all_to_all | solution.py:40
  108.7 4.5 %all-to-all-start.5 = ((f32[4,64,1024]{2,1,0:T(8,128)}), f32[4,64,1024]{2,1,0:T(8,128)S(1)}, u32[]{:S(2)}, u32[]{:S(2)}) async-start(f32[4,64,1024]{2,1,0:T(8,128)} %bitcast.8), calls=%async_computation.5 | async-start | bytes 2097152 | tf_op jit(solution)/shard_map/all_to_all | solution.py:40
  114.5 0.0 copy-start.3
  114.5 0.6 copy-done.3
  115.2 0.7 reduce_sum.9
  115.9 0.7 fusion.10
  119.2 0.6 gather_fusion.1
  119.8 1.2 broadcast_select_fusion.1
  121.0 0.0 copy-start
  121.0 5.8 %all-to-all-done.5 = f32[4,64,1024]{2,1,0:T(8,128)S(1)} async-done(((f32[4,64,1024]{2,1,0:T(8,128)}), f32[4,64,1024]{2,1,0:T(8,128)S(1)}, u32[]{:S(2)}, u32[]{:S(2)}) %all-to-all-start.5) | async-done | bytes 1048608 | tf_op jit(solution)/shard_map/all_to_all | solution.py:40
  126.8 0.0 copy-start.1
  126.8 1.0 copy-done.1
  127.8 4.4 %all-to-all-start.3 = ((f32[4,64,1024]{2,1,0:T(8,128)}), f32[4,64,1024]{2,1,0:T(8,128)S(1)}, u32[]{:S(2)}, u32[]{:S(2)}) async-start(f32[4,64,1024]{2,1,0:T(8,128)} %broadcast_select_fusion.1), calls=%async_computation.3 | async-start | bytes 2097152 | tf_op jit(solution)/shard_map/all_to_all | solution.py:42
  133.6 0.0 copy-done
  133.6 1.0 fusion.9
  134.7 1.8 %gather_fusion.3 = f32[4,64,1024]{2,1,0:T(8,128)S(1)} fusion(f32[4,64,1024]{2,1,0:T(8,128)} %copy-done.1, s32[1024]{0:T(1024)S(1)} %pad_clamp_fusion), kind=kCustom, calls=%fused_computation.3.clone | custom fusion | bytes 2097168 | tf_op jit(solution)/shard_map/jit(_take)/gather | solution.py:28
  136.5 1.2 broadcast_select_fusion
  137.7 8.0 %all-to-all-done.3 = f32[4,64,1024]{2,1,0:T(8,128)S(1)} async-done(((f32[4,64,1024]{2,1,0:T(8,128)}), f32[4,64,1024]{2,1,0:T(8,128)S(1)}, u32[]{:S(2)}, u32[]{:S(2)}) %all-to-all-start.3) | async-done | bytes 1048608 | tf_op jit(solution)/shard_map/all_to_all | solution.py:42
  145.7 4.4 %all-to-all-start.6 = ((f32[4,64,1024]{2,1,0:T(8,128)}), f32[4,64,1024]{2,1,0:T(8,128)S(1)}, u32[]{:S(2)}, u32[]{:S(2)}) async-start(f32[4,64,1024]{2,1,0:T(8,128)} %broadcast_select_fusion), calls=%async_computation.6 | async-start | bytes 2097152 | tf_op jit(solution)/shard_map/all_to_all | solution.py:42
  150.1 1.0 fusion.12
  151.1 1.0 fusion.5
  152.2 2.0 %convolution_add_fusion.1 = f32[256,1024]{1,0:T(8,128)} fusion(f32[256,1024]{1,0:T(8,128)S(1)} %fusion.12, f32[256,256]{1,0:T(8,128)S(1)} %fusion.5, f32[256,1024]{1,0:T(8,128)S(1)} %bitcast.24), kind=kOutput, calls=%fused_computation.5 | convolution fusion | flops 805568512 | bytes 3407872 | tf_op jit(solution)/shard_map/dot_general | solution.py:22
  154.2 9.5 %all-to-all-done.6 = f32[4,64,1024]{2,1,0:T(8,128)S(1)} async-done(((f32[4,64,1024]{2,1,0:T(8,128)}), f32[4,64,1024]{2,1,0:T(8,128)S(1)}, u32[]{:S(2)}, u32[]{:S(2)}) %all-to-all-start.6) | async-done | bytes 1048608 | tf_op jit(solution)/shard_map/all_to_all | solution.py:42
  163.7 0.0 copy-start.2
  163.7 1.0 fusion.2
  164.7 0.2 copy-done.2
  164.9 2.0 %convolution_add_fusion = f32[256,1024]{1,0:T(8,128)} fusion(f32[256,1024]{1,0:T(8,128)S(1)} %copy-done.2, f32[256,256]{1,0:T(8,128)S(1)} %fusion.2, f32[256,1024]{1,0:T(8,128)S(1)} %bitcast.26), kind=kOutput, calls=%fused_computation.4 | convolution fusion | flops 805568512 | bytes 3407872 | tf_op jit(solution)/shard_map/dot_general | solution.py:22
  (12 shorter events, 0.1 us)
Async XLA Ops:
  0.0 5.9 %copy-start.4 = (s32[2]{0:T(128)S(1)}, s32[2]{0:T(128)}, u32[]{:S(2)}) copy-start(s32[2]{0:T(128)} %param.9) | copy-start | bytes 28
  0.0 28.8 %all-to-all-start = ((f32[8,32,1024]{2,1,0:T(8,128)}), f32[8,32,1024]{2,1,0:T(8,128)S(1)}, u32[]{:S(2)}, u32[]{:S(2)}) async-start(f32[8,32,1024]{2,1,0:T(8,128)} %bitcast.22), calls=%async_computation | async-start | bytes 2097152 | tf_op jit(solution)/shard_map/all_to_all | solution.py:33
  30.5 29.9 %all-to-all-start.1 = ((f32[8,32,1024]{2,1,0:T(8,128)}), f32[8,32,1024]{2,1,0:T(8,128)S(1)}, u32[]{:S(2)}, u32[]{:S(2)}) async-start(f32[8,32,1024]{2,1,0:T(8,128)} %broadcast_select_fusion.3), calls=%async_computation.1 | async-start | bytes 2097152 | tf_op jit(solution)/shard_map/all_to_all | solution.py:35
  108.7 18.1 %all-to-all-start.5 = ((f32[4,64,1024]{2,1,0:T(8,128)}), f32[4,64,1024]{2,1,0:T(8,128)S(1)}, u32[]{:S(2)}, u32[]{:S(2)}) async-start(f32[4,64,1024]{2,1,0:T(8,128)} %bitcast.8), calls=%async_computation.5 | async-start | bytes 2097152 | tf_op jit(solution)/shard_map/all_to_all | solution.py:40
  114.5 0.7 copy-start.3
  121.0 12.6 %copy-start = (f32[256,1024]{1,0:T(8,128)S(1)}, f32[256,1024]{1,0:T(8,128)}, u32[]{:S(2)}) copy-start(f32[256,1024]{1,0:T(8,128)} %param.7) | copy-start | bytes 3145732
  126.8 1.0 copy-start.1
  127.8 18.0 %all-to-all-start.3 = ((f32[4,64,1024]{2,1,0:T(8,128)}), f32[4,64,1024]{2,1,0:T(8,128)S(1)}, u32[]{:S(2)}, u32[]{:S(2)}) async-start(f32[4,64,1024]{2,1,0:T(8,128)} %broadcast_select_fusion.1), calls=%async_computation.3 | async-start | bytes 2097152 | tf_op jit(solution)/shard_map/all_to_all | solution.py:42
  145.7 18.0 %all-to-all-start.6 = ((f32[4,64,1024]{2,1,0:T(8,128)}), f32[4,64,1024]{2,1,0:T(8,128)S(1)}, u32[]{:S(2)}, u32[]{:S(2)}) async-start(f32[4,64,1024]{2,1,0:T(8,128)} %broadcast_select_fusion), calls=%async_computation.6 | async-start | bytes 2097152 | tf_op jit(solution)/shard_map/all_to_all | solution.py:42
  163.7 1.2 copy-start.2
where the time goes:
time: 170 us; the launch traced here: 167 us
  waiting for transfers between devices  62.6 us (37%)
  blocking collectives  48.2 us (28%)
  starting transfers between devices  25.7 us (15%)
  between operations  10.9 us (6%)
  matrix products  8.17 us (5%)
  local copies, waits for them, and re-layouts  6.83 us (4%)
  other arithmetic  4.46 us (3%)
    all_to_all x1, blocking collectives, fetch_across(): return lax.all_to_all(chosen, 'gx', split_axis=0, concat_axis=0, tiled=True)  30.1 us
    all_to_all x1, waiting for transfers between devices, fetch_across(): lax.all_to_all(block, 'gx', split_axis=0, concat_axis=0, tiled=True)  19.7 us
    all_to_all x1, waiting for transfers between devices, fetch_across(): return lax.all_to_all(chosen, 'gx', split_axis=0, concat_axis=0, tiled=True)  19.7 us
    all_to_all x1, blocking collectives, fetch_down(): lax.all_to_all(block, 'gy', split_axis=0, concat_axis=0, tiled=True)  18.1 us
    all_to_all x2, waiting for transfers between devices, fetch_down(): return lax.all_to_all(chosen, 'gy', split_axis=0, concat_axis=0, tiled=True)  17.5 us
    all_to_all x2, starting transfers between devices, fetch_down(): return lax.all_to_all(chosen, 'gy', split_axis=0, concat_axis=0, tiled=True)  8.71 us
    all_to_all x1, starting transfers between devices, fetch_across(): return lax.all_to_all(chosen, 'gx', split_axis=0, concat_axis=0, tiled=True)  6.63 us
    all_to_all x1, starting transfers between devices, fetch_across(): lax.all_to_all(block, 'gx', split_axis=0, concat_axis=0, tiled=True)  5.85 us
  transfers between devices with their start and end apart: 5, of which 5 were waited for; matrix products, arithmetic and copies ran while one was open for 8% of the time, Pallas kernels for 0%

commit v1 on v0

v1 whole, which is shorter than its diff:
```python
import functools

import jax
import jax.numpy as jnp
from jax import lax
from jax.experimental import pallas as pl
from jax.experimental.pallas import tpu as pltpu
from jax.sharding import PartitionSpec as P

MESH = pl.DeviceIdType.MESH
CHUNKS = 8
GROUPS = 2
KERNEL_DEVICES = 64


def pair_weight(label_own, label_other, real_rows, fake_rows, loss_scale):
    both_real = loss_scale / (real_rows * (real_rows - 1.0))
    both_fake = loss_scale / (fake_rows * (fake_rows - 1.0))
    mixed = -loss_scale / (real_rows * fake_rows)
    same = label_own == label_other
    return jnp.where(same, jnp.where(label_own == 1, both_real, both_fake), mixed)


def flipped(index, mask):
    result = index
    bit = 1
    while bit <= mask:
        if mask & bit:
            result = result + bit * (1 - 2 * ((index // bit) % 2))
        bit *= 2
    return result


def split(values):
    high = values.astype(jnp.bfloat16)
    low = (values - high.astype(jnp.float32)).astype(jnp.bfloat16)
    return high, low


def dot_t(left, right):
    return lax.dot_general(
        left, right, (((1,), (1,)), ((), ())), preferred_element_type=jnp.float32
    )


def dot(left, right):
    return jnp.dot(left, right, preferred_element_type=jnp.float32)


def exchange_kernel(
    mask, across, down, labels_ref, block_ref, grad_ref, held, own_high, own_low,
    load_sem, send_near, recv_near, send_far, recv_far,
):
    rows, width = block_ref.shape
    blocks = across * down
    chunk = rows // CHUNKS
    group = rows // GROUPS
    own = lax.axis_index("gx") * down + lax.axis_index("gy")
    near = flipped(own, mask)
    far = flipped(own, (blocks - 1) ^ mask)
    flip = flipped(own, blocks - 1)

    def device(index):
        return (index // down, index % down)

    load = pltpu.make_async_copy(block_ref, held.at[pl.ds(0, rows)], load_sem)
    load.start()

    barrier = pltpu.get_barrier_semaphore()
    for peer in (near, far):
        pl.semaphore_signal(barrier, inc=1, device_id=device(peer), device_id_type=MESH)
    pl.semaphore_wait(barrier, 2)

    def to_near(at):
        return pltpu.make_async_remote_copy(
            src_ref=block_ref.at[pl.ds(at * chunk, chunk)],
            dst_ref=held.at[pl.ds(rows + at * chunk, chunk)],
            send_sem=send_near.at[at],
            recv_sem=recv_near.at[at],
            device_id=device(near),
            device_id_type=MESH,
        )

    def to_far(at):
        return pltpu.make_async_remote_copy(
            src_ref=held.at[pl.ds(rows + at * chunk, chunk)],
            dst_ref=held.at[pl.ds(2 * rows + at * chunk, chunk)],
            send_sem=send_far.at[at],
            recv_sem=recv_far.at[at],
            device_id=device(far),
            device_id_type=MESH,
        )

    def each(first, count, body):
        def step(at, carry):
            body(first + at)
            return carry

        lax.fori_loop(0, count, step, 0)

    each(0, CHUNKS, lambda at: to_near(at).start())

    label_sum = lax.fori_loop(
        0, blocks, lambda at, total: total + labels_ref[at], jnp.int32(0)
    )
    all_rows = rows * blocks
    real_rows = (label_sum * rows).astype(jnp.float32)
    fake_rows = jnp.float32(all_rows) - real_rows
    loss_scale = float(all_rows) * float(all_rows) / 16.0
    label_own = labels_ref[own]
    root_width = float(width) ** 0.5
    weights = [
        pair_weight(label_own, label, real_rows, fake_rows, loss_scale) * (6.0 / root_width)
        for label in (label_own, labels_ref[near], labels_ref[flip])
    ]

    load.wait()

    def prepare(at):
        here = pl.ds(at * chunk, chunk)
        high, low = split(held[here, :])
        own_high[here, :] = high
        own_low[here, :] = low
        grad_ref[here, :] = jnp.zeros((chunk, width), jnp.float32)

    each(0, CHUNKS, prepare)

    def relay(at):
        to_near(at).wait_recv()
        to_far(at).start()

    def tile(at, carry):
        which = at // GROUPS
        each(at + which * (2 * at - 4), (2 + 9 * which - 5 * which * which) // 2, relay)
        each(
            (CHUNKS // GROUPS) * (at % GROUPS),
            (CHUNKS // GROUPS) * (which // 2),
            lambda piece: to_far(piece).wait_recv(),
        )
        high, low = split(held[pl.ds(at * group, group), :])
        scores = (
            dot_t(own_high[...], high) + dot_t(own_high[...], low) + dot_t(own_low[...], high)
        ) * (1.0 / root_width)
        weight = jnp.where(which == 0, weights[0], jnp.where(which == 1, weights[1], weights[2]))
        raised = scores + 1.0
        coefficient = weight * (raised * raised)
        row = lax.broadcasted_iota(jnp.int32, (rows, group), 0)
        column = lax.broadcasted_iota(jnp.int32, (rows, group), 1) + at * group
        coefficient = jnp.where(row == column, 0.0, coefficient)
        c_high, c_low = split(coefficient)
        step = 256
        for start in range(0, width, step):
            here = slice(start, start + step)
            grad_ref[:, here] += (
                dot(c_high, high[:, here]) + dot(c_high, low[:, here]) + dot(c_low, high[:, here])
            )
        return carry

    lax.fori_loop(0, 3 * GROUPS, tile, 0)

    def finish(at):
        to_near(at).wait_send()
        to_far(at).wait_send()

    each(0, CHUNKS, finish)


def by_kernel(features, labels, mask, across, down):
    rows, width = features.shape
    blocks = across * down

    def branch(value):
        def call(features, labels):
            return pl.pallas_call(
                functools.partial(exchange_kernel, value, across, down),
                out_shape=jax.ShapeDtypeStruct((rows, width), jnp.float32),
                in_specs=[
                    pl.BlockSpec(memory_space=pltpu.SMEM),
                    pl.BlockSpec(memory_space=pl.ANY),
                ],
                out_specs=pl.BlockSpec(memory_space=pltpu.VMEM),
                scratch_shapes=[
                    pltpu.VMEM((3 * rows, width), jnp.float32),
                    pltpu.VMEM((rows, width), jnp.bfloat16),
                    pltpu.VMEM((rows, width), jnp.bfloat16),
                    pltpu.SemaphoreType.DMA,
                    pltpu.SemaphoreType.DMA((CHUNKS,)),
                    pltpu.SemaphoreType.DMA((CHUNKS,)),
                    pltpu.SemaphoreType.DMA((CHUNKS,)),
                    pltpu.SemaphoreType.DMA((CHUNKS,)),
                ],
                compiler_params=pltpu.CompilerParams(
                    collective_id=value,
                    has_side_effects=True,
                    vmem_limit_bytes=32 * 1024 * 1024,
                ),
                cost_estimate=pl.CostEstimate(
                    flops=36 * rows * rows * width,
                    bytes_accessed=12 * rows * width,
                    transcendentals=0,
                ),
                name="mmd_mask_%d" % value,
            )(labels, features)

        return call

    return lax.switch(
        mask - 1, [branch(value) for value in range(1, blocks - 1)], features, labels
    )


def tile_grad(own_rows, partner, weight, skip_diag):
    row_count, feat_width = own_rows.shape
    root_width = jnp.sqrt(jnp.float32(feat_width))
    scores = jnp.dot(own_rows, partner.T, precision=lax.Precision.HIGHEST) / root_width
    coefficient = weight * (6.0 / root_width) * (scores + 1.0) ** 2
    if skip_diag:
        coefficient = jnp.where(jnp.eye(row_count, dtype=bool), jnp.float32(0.0), coefficient)
    return jnp.dot(coefficient, partner, precision=lax.Precision.HIGHEST)


def permuted(values, axis, size, mask):
    def branch(value):
        pairs = [(at, at ^ value) for at in range(size)]
        return lambda values: lax.ppermute(values, axis, pairs)

    return lax.switch(mask, [branch(value) for value in range(size)], values)


def by_permutes(features, labels, mask, across, down):
    blocks = across * down
    own = lax.axis_index("gx") * down + lax.axis_index("gy")
    near = permuted(permuted(features, "gx", across, mask // down), "gy", down, mask % down)
    pairs = [(at, blocks - 1 - at) for at in range(blocks)]
    flip = lax.ppermute(features, ("gx", "gy"), pairs)
    all_rows = features.shape[0] * blocks
    real_rows = jnp.float32(features.shape[0]) * jnp.sum(labels).astype(jnp.float32)
    fake_rows = jnp.float32(all_rows) - real_rows
    loss_scale = float(all_rows) * float(all_rows) / 16.0

    def weight(other):
        return pair_weight(labels[own], labels[other], real_rows, fake_rows, loss_scale)

    return (
        tile_grad(features, features, weight(own), True)
        + tile_grad(features, near, weight(jnp.bitwise_xor(own, mask)), False)
        + tile_grad(features, flip, weight(blocks - 1 - own), False)
    )


def solution(mesh):
    across, down = mesh.shape["gx"], mesh.shape["gy"]
    blocks = across * down

    def on_device(features, labels, rounds):
        mask = jnp.bitwise_xor(jnp.bitwise_xor(rounds[0], rounds[1]), blocks - 1)
        form = by_kernel if blocks <= KERNEL_DEVICES else by_permutes
        return form(features, labels, mask, across, down)

    return jax.shard_map(
        on_device,
        mesh=mesh,
        in_specs=(P(("gx", "gy"), None), P(), P()),
        out_specs=P(("gx", "gy"), None),
        check_vma=False,
    )
```

time: 170 us -> 65.8 us (0.39)
  the two profiles are of different devices: /device:TPU:9 before, /device:TPU:0 now
where the time goes in v1:
time: 65.8 us; the launch traced here: 65.6 us
  Pallas kernels  60.7 us (92%)
  local copies, waits for them, and re-layouts  2.86 us (4%)
  between operations  1.31 us (2%)
  loops' own time  0.72 us (1%)
    pallas_call x1, Pallas kernels, call(): pl.pallas_call(functools.partial(exchange_kernel, value, across, down), o...  60.7 us
    unnamed x5, local copies, waits for them, and re-layouts  2.28 us

profile of v1, /device:TPU:0, one launch (start us, length us, event | category | flops | bytes accessed | tf_op | source)
XLA Modules:
  0.0 65.6 jit_solution(14534699165486840469)
XLA Ops:
  0.0 0.0 copy-start
  0.0 0.7 copy-done
  0.7 0.6 fusion
  2.5 0.0 copy-start.1
  2.5 0.6 copy-done.1
  3.2 61.4 %conditional.1 = (f32[256,1024]{1,0:T(8,128)S(1)}) conditional(s32[]{:T(128)} %bitcast, (s32[32]{0:T(128)S(1)}, f32[256,1024]{1,0:T(8,128)}) %tuple.157, (s32[32]{0:T(128)S(1)}, f32[256,1024]{1,0:T(8,128)}) %tuple.158, (s32[32]{0:T(128)S(1)}, f32[256,1024]{1,0:T(8,128)}) %tuple.159, (s32[32]{0:T(128)S(1)}, ...), branch_computations={%region_0.0_spmd, %region_1.0_spmd, %region_2.0_spmd, %region_3.0_... | conditional | flops 2415919104 | bytes 3145736 | solution.py:207
  3.2 60.7 %mmd_mask_11.1 = f32[256,1024]{1,0:T(8,128)S(1)} custom-call(s32[32]{0:T(128)S(1)} %get-tuple-element.168.labels_ref, f32[256,1024]{1,0:T(8,128)} %get-tuple-element.169.block_ref), custom_call_target="tpu_custom_call" | custom-call | flops 2415919104 | bytes 3145728 | tf_op jit(solution)/shard_map/cond/branch_10_fun/mmd_mask_11/pallas_call | solution.py:174
  64.6 1.0 %copy.65 = f32[256,1024]{1,0:T(8,128)} copy(f32[256,1024]{1,0:T(8,128)S(1)} %get-tuple-element.216) | data formatting | bytes 2097152
Async XLA Ops:
  0.0 0.7 copy-start
  2.5 0.7 %copy-start.1 = (s32[32]{0:T(128)S(1)}, s32[32]{0:T(128)}, u32[]{:S(2)}) copy-start(s32[32]{0:T(128)} %param.34) | copy-start | bytes 388
